TPU v7x, 32 devices: a whole 2x2x4 slice. The times are simulated.
32 devices in a mesh: pair: 2 (over core), ctx: 4 (over y, x), head: 4 (over z).
Axes of the slice: x: 2, y: 2, z: 4, core: 2. Of those that a mesh axis runs over, the one named last changes fastest.
Arguments:
- prompt_queries: bfloat16 [512, 8192], P(('pair', 'ctx'), 'head'), may hold values from -128 to 128
- prompt_key_rows: bfloat16 [512, 1024], P(('pair', 'ctx'), 'head'), may hold values from -8 to 8
- prompt_value_rows: bfloat16 [512, 1024], P(('pair', 'ctx'), 'head'), may hold values from -6 to 6
- answer_queries: bfloat16 [2, 256, 8192], P('pair', 'ctx', 'head'), may hold values from -128 to 128
- response_key_rows: bfloat16 [2, 256, 1024], P('pair', 'ctx', 'head'), may hold values from -8 to 8
- response_value_rows: bfloat16 [2, 256, 1024], P('pair', 'ctx', 'head'), may hold values from -6 to 6
- prompt_cotangent: bfloat16 [512, 8192], P(('pair', 'ctx'), 'head'), may hold values from -6 to 6
- answer_cotangent: bfloat16 [2, 256, 8192], P('pair', 'ctx', 'head'), may hold values from -6 to 6
- prompt_length: int32 [1], replicated, may hold values from 257 to 512
- answer_lengths: int32 [2], replicated, may hold values from 129 to 256
Outputs:
- prompt_attended: bfloat16 [512, 8192], P(('pair', 'ctx'), 'head')
- answer_attended: bfloat16 [2, 256, 8192], P('pair', 'ctx', 'head')
- prompt_query_grad: bfloat16 [512, 8192], P(('pair', 'ctx'), 'head')
- prompt_key_gradient: bfloat16 [512, 1024], P(('pair', 'ctx'), 'head')
- prompt_value_gradient: bfloat16 [512, 1024], P(('pair', 'ctx'), 'head')
- answer_query_grad: bfloat16 [2, 256, 8192], P('pair', 'ctx', 'head')
- response_key_gradient: bfloat16 [2, 256, 1024], P('pair', 'ctx', 'head')
- response_value_gradient: bfloat16 [2, 256, 1024], P('pair', 'ctx', 'head')
All inputs are finite; a program needn't handle non-finite values.
Results may differ from a plain program's by a relative error of at most 0.0054.
Values may be sent and summed in bfloat16 or wider, within the bound.
A program may use at most 64 MiB of HBM per device.

v0:
```python
import jax
import jax.numpy as jnp
from jax import lax
from jax.sharding import PartitionSpec as P

QUERY_HEADS = 64
KEY_VALUE_HEADS = 8
HEAD_SIZE = 128


NEGATIVE = -1e30


def block_scores(queries, key_block, allowed, scaling):
    scores = (
        jnp.einsum("qcgd,kcd->cgqk", queries, key_block, preferred_element_type=jnp.float32)
        * scaling
    )
    return jnp.where(allowed[None, None], scores, NEGATIVE)


def statistic_block(carried, scores, allowed):
    run_max, run_sum = carried
    new_max = jnp.maximum(run_max, jnp.max(scores, axis=3))
    terms = jnp.where(allowed[None, None], jnp.exp(scores - new_max[..., None]), 0.0)
    return (new_max, run_sum * jnp.exp(run_max - new_max) + jnp.sum(terms, axis=3))


def value_block_add(accum, scores, allowed, row_max, value_block):
    probs = jnp.where(allowed[None, None], jnp.exp(scores - row_max[..., None]), 0.0).astype(
        jnp.bfloat16
    )
    return accum + jnp.einsum(
        "cgqk,kcd->cgqd", probs, value_block, preferred_element_type=jnp.float32
    )


def shares_of(scores, allowed, log_total):
    return jnp.where(allowed[None, None], jnp.exp(scores - log_total[..., None]), 0.0)


def body(
    prompt_queries,
    prompt_key_rows,
    prompt_value_rows,
    answer_queries,
    response_key_rows,
    response_value_rows,
    prompt_cotangent,
    answer_cotangent,
    prompt_length,
    answer_lengths,
):
    query_group_count = QUERY_HEADS // KEY_VALUE_HEADS
    local_heads = prompt_key_rows.shape[1] // HEAD_SIZE
    prompt_rows = prompt_queries.shape[0]
    response_row_count = answer_queries.shape[1]
    all_rows = prompt_rows + response_row_count
    ctx_devices = lax.axis_size("ctx")
    prompt_total = prompt_rows * lax.axis_size("pair") * ctx_devices
    answer_total = response_row_count * ctx_devices
    prompt_block = min(256, prompt_total)
    answer_block = min(256, answer_total)
    scaling = HEAD_SIZE ** (-0.5)
    pair_index = lax.axis_index("pair")
    ctx_index = lax.axis_index("ctx")
    prompt_len = prompt_length[0]
    answer_len = lax.dynamic_index_in_dim(answer_lengths, pair_index, keepdims=False)
    prompt_first = (pair_index * ctx_devices + ctx_index) * prompt_rows
    answer_first = ctx_index * response_row_count
    prompt_pos = prompt_first + jnp.arange(prompt_rows, dtype=jnp.int32)
    answer_pos = answer_first + jnp.arange(response_row_count, dtype=jnp.int32)
    reach = jnp.concatenate([prompt_pos, jnp.full((response_row_count,), prompt_total, jnp.int32)])
    valid_rows = jnp.concatenate([prompt_pos < prompt_len, answer_pos < answer_len])
    queries = jnp.concatenate([prompt_queries, answer_queries[0]], axis=0).reshape(
        all_rows, local_heads, query_group_count, HEAD_SIZE
    )
    later_queries = queries[prompt_rows:]
    cotangent = jnp.concatenate([prompt_cotangent, answer_cotangent[0]], axis=0).reshape(
        all_rows, local_heads, query_group_count, HEAD_SIZE
    )
    cotangent = jnp.where(valid_rows[:, None, None, None], cotangent, jnp.zeros_like(cotangent))
    later_cotangent = cotangent[prompt_rows:]
    prompt_pairs = (
        lax.all_gather(prompt_key_rows, ("pair", "ctx"), axis=0, tiled=True),
        lax.all_gather(prompt_value_rows, ("pair", "ctx"), axis=0, tiled=True),
    )
    answer_pairs = (
        lax.all_gather(response_key_rows[0], "ctx", axis=0, tiled=True),
        lax.all_gather(response_value_rows[0], "ctx", axis=0, tiled=True),
    )
    prompt_blocks = (prompt_len + prompt_block - 1) // prompt_block
    answer_blocks = (
        jnp.minimum(answer_len, answer_first + response_row_count) + answer_block - 1
    ) // answer_block

    def prompt_allowed(first_key):
        key_pos = first_key + jnp.arange(prompt_block, dtype=jnp.int32)
        return (key_pos[None, :] <= reach[:, None]) & (key_pos[None, :] < prompt_len)

    def answer_allowed(first_key):
        key_pos = first_key + jnp.arange(answer_block, dtype=jnp.int32)
        return (key_pos[None, :] <= answer_pos[:, None]) & (key_pos[None, :] < answer_len)

    def take_block(source, first_key, size):
        return lax.dynamic_slice_in_dim(source, first_key, size, 0).reshape(
            size, local_heads, HEAD_SIZE
        )

    def prompt_statistic(index, carried):
        first_key = index * prompt_block
        allowed = prompt_allowed(first_key)
        scores = block_scores(
            queries, take_block(prompt_pairs[0], first_key, prompt_block), allowed, scaling
        )
        return statistic_block(carried, scores, allowed)

    def answer_statistic(index, carried):
        first_key = index * answer_block
        allowed = answer_allowed(first_key)
        scores = block_scores(
            later_queries, take_block(answer_pairs[0], first_key, answer_block), allowed, scaling
        )
        return statistic_block(carried, scores, allowed)

    stat_shape = (local_heads, query_group_count, all_rows)
    run_max, run_sum = lax.fori_loop(
        0,
        prompt_blocks,
        prompt_statistic,
        (jnp.full(stat_shape, NEGATIVE, jnp.float32), jnp.zeros(stat_shape, jnp.float32)),
    )
    tail_max, tail_sum = lax.fori_loop(
        0,
        answer_blocks,
        answer_statistic,
        (run_max[:, :, prompt_rows:], run_sum[:, :, prompt_rows:]),
    )
    row_max = jnp.concatenate([run_max[:, :, :prompt_rows], tail_max], axis=2)
    row_total = jnp.concatenate([run_sum[:, :, :prompt_rows], tail_sum], axis=2)
    later_max = row_max[:, :, prompt_rows:]

    def prompt_values(index, accum):
        first_key = index * prompt_block
        allowed = prompt_allowed(first_key)
        scores = block_scores(
            queries, take_block(prompt_pairs[0], first_key, prompt_block), allowed, scaling
        )
        return value_block_add(
            accum, scores, allowed, row_max, take_block(prompt_pairs[1], first_key, prompt_block)
        )

    def answer_values(index, accum):
        first_key = index * answer_block
        allowed = answer_allowed(first_key)
        scores = block_scores(
            later_queries, take_block(answer_pairs[0], first_key, answer_block), allowed, scaling
        )
        return value_block_add(
            accum, scores, allowed, later_max, take_block(answer_pairs[1], first_key, answer_block)
        )

    accum = lax.fori_loop(
        0,
        prompt_blocks,
        prompt_values,
        jnp.zeros((local_heads, query_group_count, all_rows, HEAD_SIZE), jnp.float32),
    )
    tail_accum = lax.fori_loop(0, answer_blocks, answer_values, accum[:, :, prompt_rows:])
    accum = jnp.concatenate([accum[:, :, :prompt_rows], tail_accum], axis=2)
    log_total = row_max + jnp.log(row_total)
    later_total = log_total[:, :, prompt_rows:]
    output = accum / row_total[..., None]
    attended = (
        jnp.where(valid_rows[None, None, :, None], output, 0.0)
        .transpose(2, 0, 1, 3)
        .reshape(all_rows, local_heads * query_group_count * HEAD_SIZE)
        .astype(jnp.bfloat16)
    )
    row_delta = jnp.sum(cotangent.astype(jnp.float32).transpose(1, 2, 0, 3) * output, axis=3)
    later_delta = row_delta[:, :, prompt_rows:]
    back_prompt = (
        lax.all_gather(prompt_key_rows, ("pair", "ctx"), axis=0, tiled=True),
        lax.all_gather(prompt_value_rows, ("pair", "ctx"), axis=0, tiled=True),
    )
    back_answer = (
        lax.all_gather(response_key_rows[0], "ctx", axis=0, tiled=True),
        lax.all_gather(response_value_rows[0], "ctx", axis=0, tiled=True),
    )

    def backward_block(
        carried,
        first_key,
        size,
        allowed,
        key_source,
        value_source,
        rows_queries,
        rows_cotangent,
        rows_total,
        rows_delta,
    ):
        query_grad, key_grad, value_grad = carried
        key_block = take_block(key_source, first_key, size)
        value_block = take_block(value_source, first_key, size)
        scores = block_scores(rows_queries, key_block, allowed, scaling)
        shares = shares_of(scores, allowed, rows_total)
        weights = shares.astype(jnp.bfloat16)
        prob_grad = jnp.einsum(
            "qcgd,kcd->cgqk", rows_cotangent, value_block, preferred_element_type=jnp.float32
        )
        score_grad = (shares * (prob_grad - rows_delta[..., None])).astype(jnp.bfloat16)
        query_grad = query_grad + jnp.einsum(
            "cgqk,kcd->qcgd", score_grad, key_block, preferred_element_type=jnp.float32
        )
        key_part = (
            jnp.einsum(
                "cgqk,qcgd->kcd", score_grad, rows_queries, preferred_element_type=jnp.float32
            )
            * scaling
        )
        value_part = jnp.einsum(
            "cgqk,qcgd->kcd", weights, rows_cotangent, preferred_element_type=jnp.float32
        )
        key_grad = lax.dynamic_update_slice_in_dim(key_grad, key_part, first_key, 0)
        value_grad = lax.dynamic_update_slice_in_dim(value_grad, value_part, first_key, 0)
        return (query_grad, key_grad, value_grad)

    def prompt_backward(index, carried):
        first_key = index * prompt_block
        return backward_block(
            carried,
            first_key,
            prompt_block,
            prompt_allowed(first_key),
            back_prompt[0],
            back_prompt[1],
            queries,
            cotangent,
            log_total,
            row_delta,
        )

    def answer_backward(index, carried):
        first_key = index * answer_block
        return backward_block(
            carried,
            first_key,
            answer_block,
            answer_allowed(first_key),
            back_answer[0],
            back_answer[1],
            later_queries,
            later_cotangent,
            later_total,
            later_delta,
        )

    grad_shape = (all_rows, local_heads, query_group_count, HEAD_SIZE)
    query_grad, prompt_kgrad, prompt_vgrad = lax.fori_loop(
        0,
        prompt_blocks,
        prompt_backward,
        (
            jnp.zeros(grad_shape, jnp.float32),
            jnp.zeros((prompt_total, local_heads, HEAD_SIZE), jnp.float32),
            jnp.zeros((prompt_total, local_heads, HEAD_SIZE), jnp.float32),
        ),
    )
    later_qgrad, answer_kgrad, answer_vgrad = lax.fori_loop(
        0,
        answer_blocks,
        answer_backward,
        (
            jnp.zeros((response_row_count, local_heads, query_group_count, HEAD_SIZE), jnp.float32),
            jnp.zeros((answer_total, local_heads, HEAD_SIZE), jnp.float32),
            jnp.zeros((answer_total, local_heads, HEAD_SIZE), jnp.float32),
        ),
    )
    query_grad = query_grad + jnp.concatenate(
        [
            jnp.zeros((prompt_rows, local_heads, query_group_count, HEAD_SIZE), jnp.float32),
            later_qgrad,
        ],
        axis=0,
    )
    query_grad = (
        (query_grad * scaling)
        .reshape(all_rows, local_heads * query_group_count * HEAD_SIZE)
        .astype(jnp.bfloat16)
    )
    prompt_kgrad = prompt_kgrad.reshape(prompt_total, local_heads * HEAD_SIZE)
    prompt_vgrad = prompt_vgrad.reshape(prompt_total, local_heads * HEAD_SIZE)
    key_mine, value_mine = (
        lax.psum_scatter(prompt_kgrad, ("pair", "ctx"), scatter_dimension=0, tiled=True),
        lax.psum_scatter(prompt_vgrad, ("pair", "ctx"), scatter_dimension=0, tiled=True),
    )
    answer_key_mine, answer_value_mine = (
        lax.psum_scatter(
            answer_kgrad.reshape(answer_total, local_heads * HEAD_SIZE),
            "ctx",
            scatter_dimension=0,
            tiled=True,
        ),
        lax.psum_scatter(
            answer_vgrad.reshape(answer_total, local_heads * HEAD_SIZE),
            "ctx",
            scatter_dimension=0,
            tiled=True,
        ),
    )
    return (
        attended[:prompt_rows],
        attended[prompt_rows:][None],
        query_grad[:prompt_rows],
        key_mine.astype(jnp.bfloat16),
        value_mine.astype(jnp.bfloat16),
        query_grad[prompt_rows:][None],
        answer_key_mine.astype(jnp.bfloat16)[None],
        answer_value_mine.astype(jnp.bfloat16)[None],
    )


def solution(mesh):
    placed = (
        P(("pair", "ctx"), "head"),
        P(("pair", "ctx"), "head"),
        P(("pair", "ctx"), "head"),
        P("pair", "ctx", "head"),
        P("pair", "ctx", "head"),
        P("pair", "ctx", "head"),
        P(("pair", "ctx"), "head"),
        P("pair", "ctx", "head"),
        P(),
        P(),
    )
    return jax.shard_map(
        body,
        mesh=mesh,
        in_specs=placed,
        out_specs=(
            P(("pair", "ctx"), "head"),
            P("pair", "ctx", "head"),
            P(("pair", "ctx"), "head"),
            P(("pair", "ctx"), "head"),
            P(("pair", "ctx"), "head"),
            P("pair", "ctx", "head"),
            P("pair", "ctx", "head"),
            P("pair", "ctx", "head"),
        ),
        check_vma=False,
    )
```

profile of v0, /device:TPU:0, one launch (start us, length us, event | category | flops | bytes accessed | tf_op | source)
XLA Modules:
  0.0 240.5 jit_solution(11193831910891954802)
XLA Ops:
  7.9 1.3 dynamic_slice.24
  9.9 10.1 %all-gather = bf16[1,256,256]{2,1,0:T(8,128)(2,1)S(1)} all-gather(bf16[1,64,256]{2,1,0:T(8,128)(2,1)} %param.26), channel_id=2, replica_groups=mesh['pair'=2,'ctx'=4,'head'=4] {'ctx'}, dimensions={1}, use_global_device_ids=true | all-gather | bytes 163840 | tf_op jit(solution)/shard_map/all_gather | solution.py:89
  20.0 0.7 reshape.413
  20.8 8.2 %all-gather.1 = bf16[1,256,256]{2,1,0:T(8,128)(2,1)S(1)} all-gather(bf16[1,64,256]{2,1,0:T(8,128)(2,1)} %param.27), channel_id=3, replica_groups=mesh['pair'=2,'ctx'=4,'head'=4] {'ctx'}, dimensions={1}, use_global_device_ids=true | all-gather | bytes 163840 | tf_op jit(solution)/shard_map/all_gather | solution.py:90
  29.0 0.7 reshape.412
  29.8 1.0 copy.190
  30.8 23.1 %all_gather.16 = bf16[512,256]{1,0:T(8,128)(2,1)S(1)} all-gather(bf16[64,256]{1,0:T(8,128)(2,1)S(1)} %copy-done.10), channel_id=1, replica_groups=mesh['pair'=2,'ctx'=4,'head'=4] {'pair','ctx'}, dimensions={0}, use_global_device_ids=true | all-gather | bytes 294912 | tf_op jit(solution)/shard_map/all_gather | solution.py:85
  54.1 23.8 %all_gather.18 = bf16[512,256]{1,0:T(8,128)(2,1)S(1)} all-gather(bf16[64,256]{1,0:T(8,128)(2,1)S(1)} %copy-done.11), channel_id=1, replica_groups=mesh['pair'=2,'ctx'=4,'head'=4] {'pair','ctx'}, dimensions={0}, use_global_device_ids=true | all-gather | bytes 294912 | tf_op jit(solution)/shard_map/all_gather | solution.py:86
  78.5 3.9 %while.78 = (s32[]{:T(128)}, f32[2,8,128]{2,1,0:T(8,128)S(1)}, f32[2,8,128]{2,1,0:T(8,128)S(1)}, s32[]{:T(128)}, s32[128]{0:T(128)S(1)}, /*index=5*/s32[]{:T(128...) while((s32[]{:T(128)}, f32[2,8,128]{2,1,0:T(8,128)S(1)}, ...), condition=%wide.region_3.4_spmd, body=%wide.region_0.3_spmd.sunk | while | flops 138482432 | bytes 5319859 | solution.py:127
  78.5 0.7 broadcast_compare_fusion.16
  79.3 0.5 fusion.161
  79.9 0.5 select_reduce_fusion.5
  80.4 0.7 broadcast_compare_fusion.16
  81.3 0.5 fusion.161
  82.5 1.6 while.81
  82.5 0.6 broadcast_compare_fusion.19
  84.2 4.5 %while.79 = (s32[]{:T(128)}, f32[2,8,128,128]{3,2,1,0:T(8,128)S(1)}, s32[]{:T(128)}, s32[128]{0:T(128)S(1)}, s32[]{:T(128)}, /*index=5*/bf16[512,256]{0,1:T(8,12...) while((s32[]{:T(128)}, ...), condition=%wide.region_9.10_spmd, body=%wide.region_8.9_spmd.sunk | while | flops 271385344 | bytes 3484859 | solution.py:163
  84.3 0.7 broadcast_compare_fusion.17
  85.1 1.4 fusion.165
  86.5 0.7 broadcast_compare_fusion.17
  87.4 1.4 fusion.165
  88.8 1.6 copy.123
  90.4 0.7 add_compare_fusion
  91.1 0.7 slice.67
  91.9 1.0 copy.193
  92.9 1.7 copy.194
  94.6 1.4 while.82
  94.7 0.7 broadcast_compare_fusion.20
  95.5 0.6 fusion.185
  96.4 2.4 %fusion.67 = (f32[2,8,128]{1,0,2:T(2,128)S(1)}, bf16[128,2,8,128]{3,2,1,0:T(8,128)(2,1)S(1)}, bf16[128,2,8,128]{3,2,1,0:T(8,128)(2,1)}) fusion(f32[2,8,128]{1,0,2:T(2,128)S(1)} %copy.126, f32[2,8,64,128]{3,1,0,2:T(8,128)S(1)} %copy.125, f32[2,8,64,128]{3,1,0,2:T(8,128)S(1)} %slice-done, bf16[64,2,8,128]{3,2,1,0:T(8,128)(2,1)} %bitcast.369, ...), kind=kLoop, calls=%fused_computation.111 | loop fusion | flops 2357248 | bytes 2637952 | tf_op jit(solution)/shard_map/reduce_sum | solution.py:180
  99.1 0.7 broadcast.314.clone
  99.8 0.7 broadcast.314
  100.6 3.9 %while.83 = (s32[]{:T(128)}, f32[64,2,8,128]{3,0,2,1:T(8,128)S(1)}, f32[256,2,128]{2,0,1:T(8,128)}, f32[256,2,128]{2,0,1:T(8,128)}, s32[]{:T(128)}, /*index=5*/s...) while((s32[]{:T(128)}, f32[64,2,8,128]{3,0,2,1:T(8,128)S(1)}, ...), condition=%wide.wide.region_16.17_spmd.clone, body=%wide.wide.region_15.16_spmd.clone.sunk | while | flops 337871680 | bytes 7777465 | solution.py:270
  100.6 0.6 broadcast_compare_fusion.21
  101.8 1.0 convolution_bitcast_fusion.11
  103.1 1.1 fusion.199
  104.5 1.7 copy_bitcast_fusion.4
  106.3 1.7 copy_bitcast_fusion.5
  108.2 1.0 broadcast.312.clone2
  109.2 0.9 broadcast.312.clone
  110.3 11.4 %while.80 = (s32[]{:T(128)}, f32[128,2,8,128]{0,3,2,1:T(8,128)S(1)}, f32[512,2,128]{2,1,0:T(2,128)}, f32[512,2,128]{2,1,0:T(2,128)}, s32[]{:T(128)}, /*index=5*/...) while((s32[]{:T(128)}, ...), condition=%wide.region_14.15_spmd, body=%wide.region_13.14_spmd.sunk | while | flops 675676928 | bytes 24595796 | solution.py:260
  110.5 0.7 broadcast_compare_fusion.18
  111.3 0.7 fusion.176
  113.8 0.7 copy-done.1
  115.1 0.8 copy-done.2
  116.1 0.7 broadcast_compare_fusion.18
  116.9 0.7 fusion.176
  119.4 0.7 copy-done.1
  120.7 0.8 copy-done.2
  121.7 1.9 copy.221
  123.6 1.9 copy.222
  126.1 0.6 copy-done.5
  126.7 0.8 broadcast_in_dim.183
  127.5 0.8 copy.224
  128.5 0.8 broadcast_in_dim.187
  129.5 0.8 copy.223
  130.2 0.5 reduce-scatter.11.cloned.1.call-done
  130.8 1.5 convert_bitcast_fusion
  132.2 25.6 %reduce-scatter.9.cloned.1.call-done = f32[64,256]{1,0:T(8,128)} async-done(((f32[256,256]{1,0:T(8,128)}), f32[64,256]{1,0:T(8,128)}) %reduce-scatter.9.cloned.1.call-update) | async-done | bytes 65552 | tf_op jit(solution)/shard_map/reduce_scatter | solution.py:299
  157.9 1.5 convert_bitcast_fusion.1
  159.3 35.8 %reduce-scatter.7.cloned.1.call-done = f32[64,256]{1,0:T(8,128)} async-done(((f32[512,256]{1,0:T(8,128)}), f32[64,256]{1,0:T(8,128)}) %reduce-scatter.7.cloned.1.call-update) | async-done | bytes 65552 | tf_op jit(solution)/shard_map/reduce_scatter | solution.py:296
  195.1 1.5 convert_element_type.46
  196.6 35.9 %reduce-scatter.5.cloned.1.call-done = f32[64,256]{1,0:T(8,128)} async-done(((f32[512,256]{1,0:T(8,128)}), f32[64,256]{1,0:T(8,128)}) %reduce-scatter.5.cloned.1.call-update) | async-done | bytes 65552 | tf_op jit(solution)/shard_map/reduce_scatter | solution.py:295
  232.5 1.5 convert_element_type.45
  (131 shorter events, 11.8 us)
Async XLA Ops:
  7.2 23.7 %copy-start.10 = (bf16[64,256]{1,0:T(8,128)(2,1)S(1)}, bf16[64,256]{1,0:T(8,128)(2,1)}, u32[]{:S(2)}) copy-start(bf16[64,256]{1,0:T(8,128)(2,1)} %param.23) | copy-start | bytes 98308
  7.2 46.9 %copy-start.11 = (bf16[64,256]{1,0:T(8,128)(2,1)S(1)}, bf16[64,256]{1,0:T(8,128)(2,1)}, u32[]{:S(2)}) copy-start(bf16[64,256]{1,0:T(8,128)(2,1)} %param.24) | copy-start | bytes 98308
  7.2 70.9 %copy-start.7 = (bf16[1,64,2048]{2,1,0:T(8,128)(2,1)S(1)}, bf16[1,64,2048]{2,1,0:T(8,128)(2,1)}, u32[]{:S(2)}) copy-start(bf16[1,64,2048]{2,1,0:T(8,128)(2,1)} %param.25) | copy-start | bytes 786436
  7.2 123.6 %reduce-scatter.11.cloned.1.call-start = ((), (), s32[]{:S(2)}) async-start(), calls=%async_computation.7 | async-start | bytes 327680 | tf_op jit(solution)/shard_map/reduce_scatter | solution.py:305
  20.0 58.1 %copy-start = (bf16[1,256,256]{2,1,0:T(8,128)(2,1)}, bf16[1,256,256]{2,1,0:T(8,128)(2,1)S(1)}, u32[]{:S(2)}) copy-start(bf16[1,256,256]{2,1,0:T(8,128)(2,1)S(1)} %all-gather) | copy-start | bytes 393220
  29.0 49.2 %copy-start.6 = (bf16[1,256,256]{2,1,0:T(8,128)(2,1)}, bf16[1,256,256]{2,1,0:T(8,128)(2,1)S(1)}, u32[]{:S(2)}) copy-start(bf16[1,256,256]{2,1,0:T(8,128)(2,1)S(1)} %all-gather.1) | copy-start | bytes 393220
  84.1 7.0 %copy-start.12 = (f32[2,8,128]{2,1,0:T(8,128)}, f32[2,8,128]{2,1,0:T(8,128)S(1)}, u32[]{:S(2)}) copy-start(f32[2,8,128]{2,1,0:T(8,128)S(1)} %get-tuple-element.1438) | copy-start | bytes 24580
  90.4 4.2 %copy-start.8 = (bf16[256,2,128]{2,1,0:T(2,128)(2,1)S(1)}, bf16[256,2,128]{2,1,0:T(2,128)(2,1)}, u32[]{:S(2)}) copy-start(bf16[256,2,128]{2,1,0:T(2,128)(2,1)} %reshape.413) | copy-start | bytes 393220
  90.4 4.2 %copy-start.9 = (bf16[256,2,128]{2,1,0:T(2,128)(2,1)S(1)}, bf16[256,2,128]{2,1,0:T(2,128)(2,1)}, u32[]{:S(2)}) copy-start(bf16[256,2,128]{2,1,0:T(2,128)(2,1)} %reshape.412) | copy-start | bytes 393220
  94.6 1.8 slice-start
  96.4 4.1 %copy-start.14 = (f32[2,8,64]{2,1,0:T(8,128)S(1)}, f32[2,8,64]{2,1,0:T(8,128)}, u32[]{:S(2)}) copy-start(f32[2,8,64]{2,1,0:T(8,128)} %slice.67) | copy-start | bytes 12292
  106.2 4.0 %copy-start.13 = (f32[2,8,128]{2,1,0:T(8,128)S(1)}, f32[2,8,128]{2,1,0:T(8,128)}, u32[]{:S(2)}) copy-start(f32[2,8,128]{2,1,0:T(8,128)} %copy-done.12) | copy-start | bytes 24580
  106.2 51.6 %reduce-scatter.9.cloned.1.call-start = ((), (), s32[]{:S(2)}) async-start(), calls=%async_computation.6 | async-start | bytes 327680 | tf_op jit(solution)/shard_map/reduce_scatter | solution.py:299
  108.0 87.1 %reduce-scatter.7.cloned.1.call-start = ((), (), s32[]{:S(2)}) async-start(), calls=%async_computation.5 | async-start | bytes 589824 | tf_op jit(solution)/shard_map/reduce_scatter | solution.py:296
  113.4 1.0 copy-start.1
  113.4 1.2 copy-start.3
  115.1 0.8 copy-start.2
  115.1 1.0 copy-start.4
  119.0 1.0 copy-start.1
  119.1 1.2 copy-start.3
  120.7 0.8 copy-start.2
  120.7 1.0 copy-start.4
  123.6 108.9 %reduce-scatter.5.cloned.1.call-start = ((), (), s32[]{:S(2)}) async-start(), calls=%async_computation.4 | async-start | bytes 589824 | tf_op jit(solution)/shard_map/reduce_scatter | solution.py:295
  125.6 1.1 copy-start.5
Sparse Core Ops, SparseCore 0:
  106.3 24.4 reduce-scatter.10
  133.8 24.0 reduce-scatter.8
  160.9 34.1 reduce-scatter.6
  198.3 34.0 reduce-scatter.4
where the time goes:
time: 241 us; the launch traced here: 240 us
  waiting for transfers between devices  97.9 us (41%)
  blocking collectives  65.3 us (27%)
  local copies, waits for them, and re-layouts  30.2 us (13%)
  other arithmetic  17.7 us (7%)
  between operations  15.6 us (6%)
  matrix products  12.8 us (5%)
    reduce_scatter x1, waiting for transfers between devices, body(): lax.psum_scatter(prompt_kgrad, ('pair', 'ctx'), scatter_dimension=0, tile...  35.9 us
    reduce_scatter x1, waiting for transfers between devices, body(): lax.psum_scatter(prompt_vgrad, ('pair', 'ctx'), scatter_dimension=0, tile...  35.8 us
    reduce_scatter x1, waiting for transfers between devices, body(): lax.psum_scatter(answer_kgrad.reshape(answer_total, local_heads * HEAD_SI...  25.6 us
    all_gather x1, blocking collectives, body(): lax.all_gather(prompt_value_rows, ('pair', 'ctx'), axis=0, tiled=True)  23.8 us
    all_gather x1, blocking collectives, body(): lax.all_gather(prompt_key_rows, ('pair', 'ctx'), axis=0, tiled=True)  23.1 us
    all_gather x1, blocking collectives, body(): lax.all_gather(response_key_rows[0], 'ctx', axis=0, tiled=True)  10.1 us
    unnamed x33, local copies, waits for them, and re-layouts  9.84 us
    all_gather x1, blocking collectives, body(): lax.all_gather(response_value_rows[0], 'ctx', axis=0, tiled=True)  8.25 us
  transfers between devices with their start and end apart: 4, of which 4 were waited for; matrix products, arithmetic and copies ran while one was open for 10% of the time, Pallas kernels for 0%

commit v1 on v0

v1 whole, which is shorter than its diff:
```python
import functools
import math

import jax
import jax.numpy as jnp
from jax import lax
from jax.experimental import pallas as pl
from jax.experimental.pallas import tpu as pltpu
from jax.sharding import PartitionSpec as P

KEY_VALUE_HEADS = 8
HEAD_SIZE = 128
NEGATIVE = -1e30
MESH = pl.DeviceIdType.MESH
F32 = jnp.float32
BF16 = jnp.bfloat16


def greet(pairs, ctxs, p, c):
    barrier = pltpu.get_barrier_semaphore()
    for e in range(1, pairs):
        pl.semaphore_signal(
            barrier, inc=1, device_id={"pair": lax.rem(p + e, pairs)}, device_id_type=MESH
        )
    for d in range(1, ctxs):
        pl.semaphore_signal(
            barrier, inc=1, device_id={"ctx": lax.rem(c + d, ctxs)}, device_id_type=MESH
        )
    pl.semaphore_wait(barrier, pairs + ctxs - 2)


def gather_kernel(pairs, ctxs, kp, vp, kr, vr, gp, gr, send_p, recv_p, send_r, recv_r, send_f, recv_f):
    p, c = lax.axis_index("pair"), lax.axis_index("ctx")
    own = p * ctxs + c
    gp[own, 0] = kp[...]
    gp[own, 1] = vp[...]
    gr[c, 0] = kr[0]
    gr[c, 1] = vr[0]
    greet(pairs, ctxs, p, c)

    def forward(slot, e, d):
        copy = pltpu.make_async_remote_copy(
            src_ref=gp.at[slot],
            dst_ref=gp.at[slot],
            send_sem=send_f.at[e - 1, d],
            recv_sem=recv_f.at[e - 1, d],
            device_id={"pair": lax.rem(p + e, pairs)},
            device_id_type=MESH,
        )
        copy.start()
        return copy

    across, replies, forwards = [], [], []
    for d in range(1, ctxs):
        copy = pltpu.make_async_remote_copy(
            src_ref=gp.at[own],
            dst_ref=gp.at[own],
            send_sem=send_p.at[d - 1],
            recv_sem=recv_p.at[d - 1],
            device_id={"ctx": lax.rem(c + d, ctxs)},
            device_id_type=MESH,
        )
        copy.start()
        across.append(copy)
    for d in range(1, ctxs):
        copy = pltpu.make_async_remote_copy(
            src_ref=gr.at[c],
            dst_ref=gr.at[c],
            send_sem=send_r.at[d - 1],
            recv_sem=recv_r.at[d - 1],
            device_id={"ctx": lax.rem(c + d, ctxs)},
            device_id_type=MESH,
        )
        copy.start()
        replies.append(copy)
    for e in range(1, pairs):
        forwards.append(forward(own, e, 0))
    for d in range(1, ctxs):
        across[d - 1].wait_recv()
        slot = p * ctxs + lax.rem(c + ctxs - d, ctxs)
        for e in range(1, pairs):
            forwards.append(forward(slot, e, d))
    for copy in across:
        copy.wait_send()
    for copy in replies + forwards:
        copy.wait()


def gather(pairs, ctxs, kp, vp, kr, vr):
    rows, width = kp.shape
    vmem = pl.BlockSpec(memory_space=pltpu.VMEM)
    return pl.pallas_call(
        functools.partial(gather_kernel, pairs, ctxs),
        out_shape=(
            jax.ShapeDtypeStruct((pairs * ctxs, 2, rows, width), BF16),
            jax.ShapeDtypeStruct((ctxs, 2, kr.shape[1], width), BF16),
        ),
        in_specs=[vmem] * 4,
        out_specs=(vmem, vmem),
        scratch_shapes=[
            pltpu.SemaphoreType.DMA((ctxs - 1,)),
            pltpu.SemaphoreType.DMA((ctxs - 1,)),
            pltpu.SemaphoreType.DMA((ctxs - 1,)),
            pltpu.SemaphoreType.DMA((ctxs - 1,)),
            pltpu.SemaphoreType.DMA((pairs - 1, ctxs)),
            pltpu.SemaphoreType.DMA((pairs - 1, ctxs)),
        ],
        compiler_params=pltpu.CompilerParams(
            collective_id=0, has_side_effects=True, vmem_limit_bytes=32 * 2**20
        ),
    )(kp, vp, kr, vr)


def reduce_kernel(
    pairs, ctxs, tp, tr, kp, vp, kr, vr, from_pair, from_ctx, from_reply, summed,
    send_f, recv_f, send_p, recv_p, send_r, recv_r,
):
    p, c = lax.axis_index("pair"), lax.axis_index("ctx")
    own = p * ctxs + c
    greet(pairs, ctxs, p, c)
    inner, across, replies = [], [], []
    for d in list(range(1, ctxs)) + [0]:
        for e in range(1, pairs):
            q = lax.rem(p + e, pairs)
            copy = pltpu.make_async_remote_copy(
                src_ref=tp.at[q * ctxs + lax.rem(c + d, ctxs)],
                dst_ref=from_pair.at[e - 1, d],
                send_sem=send_f.at[e - 1, d],
                recv_sem=recv_f.at[e - 1, d],
                device_id={"pair": q},
                device_id_type=MESH,
            )
            copy.start()
            inner.append((d, e, copy))
    for d in range(1, ctxs):
        peer = lax.rem(c + d, ctxs)
        copy = pltpu.make_async_remote_copy(
            src_ref=tr.at[peer],
            dst_ref=from_reply.at[d - 1],
            send_sem=send_r.at[d - 1],
            recv_sem=recv_r.at[d - 1],
            device_id={"ctx": peer},
            device_id_type=MESH,
        )
        copy.start()
        replies.append(copy)

    def pair_sum(d, which):
        total = tp[p * ctxs + lax.rem(c + d, ctxs), which].astype(F32)
        for e in range(1, pairs):
            total = total + from_pair[e - 1, d, which].astype(F32)
        return total

    for d in range(1, ctxs):
        for at, _, copy in inner:
            if at == d:
                copy.wait_recv()
        for which in range(2):
            summed[d - 1, which] = pair_sum(d, which).astype(BF16)
        copy = pltpu.make_async_remote_copy(
            src_ref=summed.at[d - 1],
            dst_ref=from_ctx.at[d - 1],
            send_sem=send_p.at[d - 1],
            recv_sem=recv_p.at[d - 1],
            device_id={"ctx": lax.rem(c + d, ctxs)},
            device_id_type=MESH,
        )
        copy.start()
        across.append(copy)
    for at, _, copy in inner:
        if at == 0:
            copy.wait_recv()
    for copy in replies:
        copy.wait_recv()
    for which, out in ((0, kr), (1, vr)):
        total = tr[c, which].astype(F32)
        for d in range(1, ctxs):
            total = total + from_reply[d - 1, which].astype(F32)
        out[0] = total.astype(BF16)
    for copy in across:
        copy.wait_recv()
    for which, out in ((0, kp), (1, vp)):
        total = pair_sum(0, which)
        for d in range(1, ctxs):
            total = total + from_ctx[d - 1, which].astype(F32)
        out[...] = total.astype(BF16)
    for _, _, copy in inner:
        copy.wait_send()
    for copy in across + replies:
        copy.wait_send()


def reduce(pairs, ctxs, tp, tr):
    _, _, rows, width = tp.shape
    later = tr.shape[2]
    vmem = pl.BlockSpec(memory_space=pltpu.VMEM)
    return pl.pallas_call(
        functools.partial(reduce_kernel, pairs, ctxs),
        out_shape=(
            jax.ShapeDtypeStruct((rows, width), BF16),
            jax.ShapeDtypeStruct((rows, width), BF16),
            jax.ShapeDtypeStruct((1, later, width), BF16),
            jax.ShapeDtypeStruct((1, later, width), BF16),
        ),
        in_specs=[vmem] * 2,
        out_specs=(vmem,) * 4,
        scratch_shapes=[
            pltpu.VMEM((pairs - 1, ctxs, 2, rows, width), BF16),
            pltpu.VMEM((ctxs - 1, 2, rows, width), BF16),
            pltpu.VMEM((ctxs - 1, 2, later, width), BF16),
            pltpu.VMEM((ctxs - 1, 2, rows, width), BF16),
            pltpu.SemaphoreType.DMA((pairs - 1, ctxs)),
            pltpu.SemaphoreType.DMA((pairs - 1, ctxs)),
            pltpu.SemaphoreType.DMA((ctxs - 1,)),
            pltpu.SemaphoreType.DMA((ctxs - 1,)),
            pltpu.SemaphoreType.DMA((ctxs - 1,)),
            pltpu.SemaphoreType.DMA((ctxs - 1,)),
        ],
        compiler_params=pltpu.CompilerParams(
            collective_id=1, has_side_effects=True, vmem_limit_bytes=32 * 2**20
        ),
    )(tp, tr)


def dot(a, b):
    return lax.dot_general(a, b, (((1,), (0,)), ((), ())), preferred_element_type=F32)


def dot_nt(a, b):
    return lax.dot_general(a, b, (((1,), (1,)), ((), ())), preferred_element_type=F32)


def row_positions(first, count, rows):
    lane = lax.broadcasted_iota(jnp.int32, (1, count), 1)
    return first + lax.rem(lane, jnp.int32(rows))


def attend_block(parts, queries, cotangent, valid, scaling, grads):
    factor = scaling * math.log2(math.e)
    scores = []
    top = None
    for keys, _, _, _, limit in parts:
        s = dot_nt(keys, queries)
        at = lax.broadcasted_iota(jnp.int32, s.shape, 0)
        s = jnp.where(at <= limit, s, NEGATIVE)
        m = jnp.max(s, axis=0, keepdims=True)
        top = m if top is None else jnp.maximum(top, m)
        scores.append(s)
    terms = [jnp.exp2((s - top) * factor) for s in scores]
    total = sum(jnp.sum(t, axis=0, keepdims=True) for t in terms)
    inverse = 1.0 / total
    output = sum(dot(part[3], t.astype(BF16)) for part, t in zip(parts, terms))
    output = jnp.where(valid, output * inverse, 0.0).astype(BF16)
    prob_grads = [dot_nt(part[1], cotangent) for part in parts]
    shares = [t * inverse for t in terms]
    delta = sum(jnp.sum(w * g, axis=0, keepdims=True) for w, g in zip(shares, prob_grads))
    query_grad = None
    for part, w, g, (key_grad, value_grad, fresh) in zip(parts, shares, prob_grads, grads):
        value_add = dot(w.astype(BF16), cotangent)
        score_grad = (w * (g - delta)).astype(BF16)
        key_add = dot(score_grad, queries)
        if fresh:
            value_grad[...] = value_add
            key_grad[...] = key_add
        else:
            value_grad[...] += value_add
            key_grad[...] += key_add
        add = dot(part[2], score_grad)
        query_grad = add if query_grad is None else query_grad + add
    return output, (query_grad * scaling).astype(BF16)


def attend_kernel(
    pairs, ctxs, plen, alen, gp, gr, q, aq, do, ado,
    out, aout, dq, adq, tp, tr,
    kgrad, vgrad, kgrad_r, vgrad_r,
):
    p, c = lax.axis_index("pair"), lax.axis_index("ctx")
    slots, _, rows, size = gp.shape
    later = gr.shape[2]
    group = q.shape[1] // size
    scaling = size ** (-0.5)
    prompt_len = plen[0]
    answer_len = alen[p]
    prompt_first = (p * ctxs + c) * rows
    answer_first = c * later

    keys = gp[:, 0].reshape(slots * rows, size)
    values = gp[:, 1].reshape(slots * rows, size)
    keys_r = gr[:, 0].reshape(ctxs * later, size)
    values_r = gr[:, 1].reshape(ctxs * later, size)
    keys_t, values_t = keys.T, values.T
    keys_rt, values_rt = keys_r.T, values_r.T

    def stacked(ref, heads):
        return jnp.concatenate([ref[:, h * size : (h + 1) * size] for h in heads], axis=0)

    for answer in (False, True):
        count = later if answer else rows
        per_block = max(1, 256 // count)
        first = answer_first if answer else prompt_first
        live = answer_len if answer else prompt_len
        for start in range(0, group, per_block):
            heads = list(range(start, min(group, start + per_block)))
            lanes = len(heads) * count
            pos = row_positions(first, lanes, count)
            valid = pos < live
            queries = stacked(aq if answer else q, heads)
            cotangent = stacked(ado if answer else do, heads)
            live_row = (
                first
                + lax.rem(lax.broadcasted_iota(jnp.int32, cotangent.shape, 0), jnp.int32(count))
                < live
            )
            cotangent = jnp.where(live_row, cotangent.astype(F32), 0.0).astype(BF16)
            limit = jnp.minimum(pos, live - 1)
            if answer:
                parts = [
                    (keys, values, keys_t, values_t, jnp.full((1, lanes), prompt_len - 1, jnp.int32)),
                    (keys_r, values_r, keys_rt, values_rt, limit),
                ]
                grads = [(kgrad, vgrad, False), (kgrad_r, vgrad_r, start == 0)]
            else:
                parts = [(keys, values, keys_t, values_t, limit)]
                grads = [(kgrad, vgrad, start == 0)]
            o, g = attend_block(parts, queries, cotangent, valid, scaling, grads)
            o, g = o.T, g.T
            for i, h in enumerate(heads):
                cut, cols = slice(i * count, (i + 1) * count), slice(h * size, (h + 1) * size)
                (aout if answer else out)[:, cols] = o[cut]
                (adq if answer else dq)[:, cols] = g[cut]
    tp[:, 0] = (kgrad[...] * scaling).astype(BF16).reshape(slots, rows, size)
    tp[:, 1] = vgrad[...].astype(BF16).reshape(slots, rows, size)
    tr[:, 0] = (kgrad_r[...] * scaling).astype(BF16).reshape(ctxs, later, size)
    tr[:, 1] = vgrad_r[...].astype(BF16).reshape(ctxs, later, size)


def attend(pairs, ctxs, gp, gr, q, aq, do, ado, plen, alen):
    size = HEAD_SIZE
    slots, _, rows, width = gp.shape
    later = gr.shape[2]
    heads = width // size
    cols = q.shape[1] // heads
    smem = pl.BlockSpec(memory_space=pltpu.SMEM)
    kv = pl.BlockSpec((slots, 2, rows, size), lambda h: (0, 0, 0, h))
    kv_r = pl.BlockSpec((ctxs, 2, later, size), lambda h: (0, 0, 0, h))
    flat = pl.BlockSpec((rows, cols), lambda h: (0, h))
    deep = pl.BlockSpec((None, later, cols), lambda h: (0, 0, h))
    return pl.pallas_call(
        functools.partial(attend_kernel, pairs, ctxs),
        grid=(heads,),
        out_shape=(
            jax.ShapeDtypeStruct(q.shape, BF16),
            jax.ShapeDtypeStruct(aq.shape, BF16),
            jax.ShapeDtypeStruct(q.shape, BF16),
            jax.ShapeDtypeStruct(aq.shape, BF16),
            jax.ShapeDtypeStruct(gp.shape, BF16),
            jax.ShapeDtypeStruct(gr.shape, BF16),
        ),
        in_specs=[smem, smem, kv, kv_r, flat, deep, flat, deep],
        out_specs=(flat, deep, flat, deep, kv, kv_r),
        scratch_shapes=[
            pltpu.VMEM((slots * rows, size), F32),
            pltpu.VMEM((slots * rows, size), F32),
            pltpu.VMEM((ctxs * later, size), F32),
            pltpu.VMEM((ctxs * later, size), F32),
        ],
        compiler_params=pltpu.CompilerParams(vmem_limit_bytes=56 * 2**20),
    )(plen, alen, gp, gr, q, aq, do, ado)


def body(pairs, ctxs, q, kp, vp, aq, kr, vr, do, ado, plen, alen):
    gp, gr = gather(pairs, ctxs, kp, vp, kr, vr)
    out, aout, dq, adq, tp, tr = attend(pairs, ctxs, gp, gr, q, aq, do, ado, plen, alen)
    dkp, dvp, dkr, dvr = reduce(pairs, ctxs, tp, tr)
    return out, aout, dq, dkp, dvp, adq, dkr, dvr


def solution(mesh):
    flat = P(("pair", "ctx"), "head")
    deep = P("pair", "ctx", "head")
    return jax.shard_map(
        functools.partial(body, mesh.shape["pair"], mesh.shape["ctx"]),
        mesh=mesh,
        in_specs=(flat, flat, flat, deep, deep, deep, flat, deep, P(), P()),
        out_specs=(flat, deep, flat, flat, flat, deep, deep, deep),
        check_vma=False,
    )
```

time: 241 us -> 40.6 us (0.17)
  waiting for transfers between devices: 97.9 us -> 0 us
  blocking collectives: 65.3 us -> 0 us
  Pallas kernels: 0 us -> 29.8 us
  local copies, waits for them, and re-layouts: 30.2 us -> 8.96 us
  other arithmetic: 17.7 us -> 0 us
  between operations: 15.6 us -> 1.33 us
  matrix products: 12.8 us -> 0 us
    reduce_scatter x4 -> x0, waiting for transfers between devices: 97.9 us -> none  [the longest x1 35.9 us: body(): lax.psum_scatter(prompt_kgrad, ('pair', 'ctx'), scatter_dimension=0, tile...]
    all_gather x4 -> x0, blocking collectives: 65.3 us -> none  [the longest x1 23.8 us: body(): lax.all_gather(prompt_value_rows, ('pair', 'ctx'), axis=0, tiled=True)]
    pallas_call x0 -> x3, Pallas kernels: none -> 29.8 us  [the longest x1 10.7 us: gather(): pl.pallas_call(functools.partial(gather_kernel, pairs, ctxs), out_shape=(...]
    dot_general x21 -> x0, matrix products: 12.8 us -> none  [the longest x3 3.35 us: value_block_add(): jnp.einsum('cgqk,kcd->cgqd', probs, value_block, preferred_element_type=j...]
    lt x10 -> x0, other arithmetic: 6.51 us -> none  [the longest x6 3.92 us: prompt_allowed(): key_pos[None, :] < prompt_len]
    while x27 -> x0, local copies, waits for them, and re-layouts: 6.5 us -> none
    reshape x7 -> x0, local copies, waits for them, and re-layouts: 4.86 us -> none  [the longest x1 1.68 us: body(): answer_vgrad.reshape(answer_total, local_heads * HEAD_SIZE)]
    reduce_sum x4 -> x0, other arithmetic: 3.87 us -> none  [the longest x1 2.44 us: body(): jnp.sum(cotangent.astype(jnp.float32).transpose(1, 2, 0, 3) * output, axi...]
  transfers between devices with their start and end apart: 4 -> 0, of which waited for: 4 -> 0; matrix products, arithmetic and copies ran while one was open for 10% -> 0% of each run, Pallas kernels for 0% -> 0%
where the time goes in v1:
time: 40.6 us; the launch traced here: 40.1 us
  Pallas kernels  29.8 us (73%)
  local copies, waits for them, and re-layouts  8.96 us (22%)
  between operations  1.33 us (3%)
    pallas_call x1, Pallas kernels, gather(): pl.pallas_call(functools.partial(gather_kernel, pairs, ctxs), out_shape=(...  10.7 us
    pallas_call x1, Pallas kernels, attend(): pl.pallas_call(functools.partial(attend_kernel, pairs, ctxs), grid=(heads...  10.1 us
    pallas_call x1, Pallas kernels, reduce(): pl.pallas_call(functools.partial(reduce_kernel, pairs, ctxs), out_shape=(...  9.03 us
    unnamed x20, local copies, waits for them, and re-layouts  8.96 us

profile of v1, /device:TPU:0, one launch (start us, length us, event | category | flops | bytes accessed | tf_op | source)
XLA Modules:
  0.0 40.1 jit_solution(5840790839158537315)
XLA Ops:
  1.3 0.0 copy-start.4
  1.3 0.7 %copy-done.4 = bf16[64,256]{1,0:T(8,128)(2,1)S(1)} copy-done((bf16[64,256]{1,0:T(8,128)(2,1)S(1)}, bf16[64,256]{1,0:T(8,128)(2,1)}, u32[]{:S(2)}) %copy-start.4) | copy-done | bytes 32792
  2.0 0.0 copy-start.5
  2.0 0.8 %copy-done.5 = bf16[64,256]{1,0:T(8,128)(2,1)S(1)} copy-done((bf16[64,256]{1,0:T(8,128)(2,1)S(1)}, bf16[64,256]{1,0:T(8,128)(2,1)}, u32[]{:S(2)}) %copy-start.5) | copy-done | bytes 32792
  2.8 0.0 copy-start.6
  2.8 0.8 %copy-done.6 = bf16[1,64,256]{2,1,0:T(8,128)(2,1)S(1)} copy-done((bf16[1,64,256]{2,1,0:T(8,128)(2,1)S(1)}, bf16[1,64,256]{2,1,0:T(8,128)(2,1)}, u32[]{:S(2)}) %copy-start.6) | copy-done | bytes 32792
  3.6 0.0 copy-start.7
  3.6 0.8 %copy-done.7 = bf16[1,64,256]{2,1,0:T(8,128)(2,1)S(1)} copy-done((bf16[1,64,256]{2,1,0:T(8,128)(2,1)S(1)}, bf16[1,64,256]{2,1,0:T(8,128)(2,1)}, u32[]{:S(2)}) %copy-start.7) | copy-done | bytes 32792
  4.3 10.7 %shard_map.161 = (bf16[8,2,64,256]{3,2,1,0:T(8,128)(2,1)S(1)}, bf16[4,2,64,256]{3,2,1,0:T(8,128)(2,1)S(1)}) custom-call(bf16[64,256]{1,0:T(8,128)(2,1)S(1)} %copy-done.4, bf16[64,256]{1,0:T(8,128)(2,1)S(1)} %copy-done.5, bf16[1,64,256]{2,1,0:T(8,128)(2,1)S(1)} %copy-done.6, bf16[1,64,256]{2,1,0:T(8,128)(2,1)S(1)} %copy-done.7), custom_call_target="tpu_custom_call" | custom-call | tf_op jit(solution)/shard_map/pallas_call | solution.py:92
  15.0 0.0 copy-start
  15.0 0.8 %copy-done = bf16[8,2,64,256]{3,2,1,0:T(8,128)(2,1)} copy-done((bf16[8,2,64,256]{3,2,1,0:T(8,128)(2,1)}, bf16[8,2,64,256]{3,2,1,0:T(8,128)(2,1)S(1)}, u32[]{:S(2)}) %copy-start) | copy-done | bytes 524312
  15.8 0.0 copy-start.3
  15.8 0.7 %copy-done.3 = bf16[4,2,64,256]{3,2,1,0:T(8,128)(2,1)} copy-done((bf16[4,2,64,256]{3,2,1,0:T(8,128)(2,1)}, bf16[4,2,64,256]{3,2,1,0:T(8,128)(2,1)S(1)}, u32[]{:S(2)}) %copy-start.3) | copy-done | bytes 262168
  16.5 10.1 %shard_map.162 = (bf16[64,2048]{1,0:T(8,128)(2,1)}, bf16[1,64,2048]{2,1,0:T(8,128)(2,1)}, bf16[64,2048]{1,0:T(8,128)(2,1)}, bf16[1,64,2048]{2,1,0:T(8,128)(2,1)}...) custom-call(s32[1]{0:T(128)S(6)} %copy.22.plen, s32[2]{0:T(128)} %alen.1, ...), custom_call_target="tpu_custom_call" | custom-call | tf_op jit(solution)/shard_map/pallas_call | solution.py:349
  26.6 0.0 copy-start.1
  26.6 1.0 %copy-done.1 = bf16[8,2,64,256]{3,2,1,0:T(8,128)(2,1)S(1)} copy-done((bf16[8,2,64,256]{3,2,1,0:T(8,128)(2,1)S(1)}, bf16[8,2,64,256]{3,2,1,0:T(8,128)(2,1)}, u32[]{:S(2)}) %copy-start.1) | copy-done | bytes 524312
  27.6 0.0 copy-start.2
  27.6 0.9 %copy-done.2 = bf16[4,2,64,256]{3,2,1,0:T(8,128)(2,1)S(1)} copy-done((bf16[4,2,64,256]{3,2,1,0:T(8,128)(2,1)S(1)}, bf16[4,2,64,256]{3,2,1,0:T(8,128)(2,1)}, u32[]{:S(2)}) %copy-start.2) | copy-done | bytes 262168
  28.6 9.0 %shard_map.163 = (bf16[64,256]{1,0:T(8,128)(2,1)S(1)}, bf16[64,256]{1,0:T(8,128)(2,1)S(1)}, bf16[1,64,256]{2,1,0:T(8,128)(2,1)S(1)}, bf16[1,64,256]{2,1,0:T(8,128)(2,1)S(1)}) custom-call(bf16[8,2,64,256]{3,2,1,0:T(8,128)(2,1)S(1)} %copy-done.1, bf16[4,2,64,256]{3,2,1,0:T(8,128)(2,1)S(1)} %copy-done.2), custom_call_target="tpu_custom_call" | custom-call | tf_op jit(solution)/shard_map/pallas_call | solution.py:197
  37.6 0.6 %copy.23 = bf16[64,256]{1,0:T(8,128)(2,1)} copy(bf16[64,256]{1,0:T(8,128)(2,1)S(1)} %get-tuple-element.43) | data formatting | bytes 65536
  38.2 0.6 %copy.24 = bf16[64,256]{1,0:T(8,128)(2,1)} copy(bf16[64,256]{1,0:T(8,128)(2,1)S(1)} %get-tuple-element.44) | data formatting | bytes 65536
  38.9 0.6 %copy.25 = bf16[1,64,256]{2,1,0:T(8,128)(2,1)} copy(bf16[1,64,256]{2,1,0:T(8,128)(2,1)S(1)} %get-tuple-element.46) | data formatting | bytes 65536
  39.5 0.6 %copy.26 = bf16[1,64,256]{2,1,0:T(8,128)(2,1)} copy(bf16[1,64,256]{2,1,0:T(8,128)(2,1)S(1)} %get-tuple-element.47) | data formatting | bytes 65536
Async XLA Ops:
  1.3 0.8 %copy-start.4 = (bf16[64,256]{1,0:T(8,128)(2,1)S(1)}, bf16[64,256]{1,0:T(8,128)(2,1)}, u32[]{:S(2)}) copy-start(bf16[64,256]{1,0:T(8,128)(2,1)} %kp.1) | copy-start | bytes 98308
  2.0 0.8 %copy-start.5 = (bf16[64,256]{1,0:T(8,128)(2,1)S(1)}, bf16[64,256]{1,0:T(8,128)(2,1)}, u32[]{:S(2)}) copy-start(bf16[64,256]{1,0:T(8,128)(2,1)} %vp.1) | copy-start | bytes 98308
  2.8 0.8 %copy-start.6 = (bf16[1,64,256]{2,1,0:T(8,128)(2,1)S(1)}, bf16[1,64,256]{2,1,0:T(8,128)(2,1)}, u32[]{:S(2)}) copy-start(bf16[1,64,256]{2,1,0:T(8,128)(2,1)} %kr.1) | copy-start | bytes 98308
  3.6 0.8 %copy-start.7 = (bf16[1,64,256]{2,1,0:T(8,128)(2,1)S(1)}, bf16[1,64,256]{2,1,0:T(8,128)(2,1)}, u32[]{:S(2)}) copy-start(bf16[1,64,256]{2,1,0:T(8,128)(2,1)} %vr.1) | copy-start | bytes 98308
  15.0 0.8 %copy-start = (bf16[8,2,64,256]{3,2,1,0:T(8,128)(2,1)}, bf16[8,2,64,256]{3,2,1,0:T(8,128)(2,1)S(1)}, u32[]{:S(2)}) copy-start(bf16[8,2,64,256]{3,2,1,0:T(8,128)(2,1)S(1)} %get-tuple-element.20.gp) | copy-start | bytes 1572868
  15.8 0.7 %copy-start.3 = (bf16[4,2,64,256]{3,2,1,0:T(8,128)(2,1)}, bf16[4,2,64,256]{3,2,1,0:T(8,128)(2,1)S(1)}, u32[]{:S(2)}) copy-start(bf16[4,2,64,256]{3,2,1,0:T(8,128)(2,1)S(1)} %get-tuple-element.21.gr) | copy-start | bytes 786436
  26.6 1.0 %copy-start.1 = (bf16[8,2,64,256]{3,2,1,0:T(8,128)(2,1)S(1)}, bf16[8,2,64,256]{3,2,1,0:T(8,128)(2,1)}, u32[]{:S(2)}) copy-start(bf16[8,2,64,256]{3,2,1,0:T(8,128)(2,1)} %get-tuple-element.25.tp) | copy-start | bytes 1572868
  27.6 0.9 %copy-start.2 = (bf16[4,2,64,256]{3,2,1,0:T(8,128)(2,1)S(1)}, bf16[4,2,64,256]{3,2,1,0:T(8,128)(2,1)}, u32[]{:S(2)}) copy-start(bf16[4,2,64,256]{3,2,1,0:T(8,128)(2,1)} %get-tuple-element.26.tr) | copy-start | bytes 786436

commit v2 on v1

v2 whole, which is shorter than its diff:
```python
import functools
import math

import jax
import jax.numpy as jnp
from jax import lax
from jax.experimental import pallas as pl
from jax.experimental.pallas import tpu as pltpu
from jax.sharding import PartitionSpec as P

KEY_VALUE_HEADS = 8
HEAD_SIZE = 128
NEGATIVE = -1e30
MESH = pl.DeviceIdType.MESH
F32 = jnp.float32
BF16 = jnp.bfloat16


def greet(pairs, ctxs, p, c):
    barrier = pltpu.get_barrier_semaphore()
    for e in range(1, pairs):
        pl.semaphore_signal(
            barrier, inc=1, device_id={"pair": lax.rem(p + e, pairs)}, device_id_type=MESH
        )
    for d in range(1, ctxs):
        pl.semaphore_signal(
            barrier, inc=1, device_id={"ctx": lax.rem(c + d, ctxs)}, device_id_type=MESH
        )
    pl.semaphore_wait(barrier, pairs + ctxs - 2)


def dot(a, b):
    return lax.dot_general(a, b, (((1,), (0,)), ((), ())), preferred_element_type=F32)


def dot_nt(a, b):
    return lax.dot_general(a, b, (((1,), (1,)), ((), ())), preferred_element_type=F32)


def row_positions(first, count, rows):
    lane = lax.broadcasted_iota(jnp.int32, (1, count), 1)
    return first + lax.rem(lane, jnp.int32(rows))


def attend_block(parts, queries, cotangent, valid, scaling, grads):
    factor = scaling * math.log2(math.e)
    scores = []
    top = None
    for keys, _, _, _, limit in parts:
        s = dot_nt(keys, queries)
        at = lax.broadcasted_iota(jnp.int32, s.shape, 0)
        s = jnp.where(at <= limit, s, NEGATIVE)
        m = jnp.max(s, axis=0, keepdims=True)
        top = m if top is None else jnp.maximum(top, m)
        scores.append(s)
    terms = [jnp.exp2((s - top) * factor) for s in scores]
    total = sum(jnp.sum(t, axis=0, keepdims=True) for t in terms)
    inverse = 1.0 / total
    output = sum(dot(part[3], t.astype(BF16)) for part, t in zip(parts, terms))
    output = jnp.where(valid, output * inverse, 0.0).astype(BF16)
    prob_grads = [dot_nt(part[1], cotangent) for part in parts]
    shares = [t * inverse for t in terms]
    delta = sum(jnp.sum(w * g, axis=0, keepdims=True) for w, g in zip(shares, prob_grads))
    query_grad = None
    for part, w, g, (key_grad, value_grad, fresh) in zip(parts, shares, prob_grads, grads):
        value_add = dot(w.astype(BF16), cotangent)
        score_grad = (w * (g - delta)).astype(BF16)
        key_add = dot(score_grad, queries)
        if fresh:
            value_grad[...] = value_add
            key_grad[...] = key_add
        else:
            value_grad[...] += value_add
            key_grad[...] += key_add
        add = dot(part[2], score_grad)
        query_grad = add if query_grad is None else query_grad + add
    return output, (query_grad * scaling).astype(BF16)


def remote(src, dst, send, recv, device):
    copy = pltpu.make_async_remote_copy(
        src_ref=src, dst_ref=dst, send_sem=send, recv_sem=recv, device_id=device, device_id_type=MESH
    )
    copy.start()
    return copy


def fused_kernel(
    pairs, ctxs, kv_heads,
    plen, alen, q, kp, vp, aq, kr, vr, do, ado,
    out, aout, dq, dkp, dvp, adq, dkr, dvr,
    gp, gr, q_v, aq_v, do_v, ado_v, out_v, aout_v, dq_v, adq_v,
    kgrad, vgrad, kgrad_r, vgrad_r, tp, tr, from_pair, from_ctx, from_reply, summed, done_p, done_r,
    load_sem, store_sem,
    g_send, g_recv, r_send, r_recv, f_send, f_recv,
    x_send, x_recv, y_send, y_recv, z_send, z_recv,
):
    p, c = lax.axis_index("pair"), lax.axis_index("ctx")
    own = p * ctxs + c
    slots = pairs * ctxs
    rows, later, size = q.shape[0], aq.shape[1], HEAD_SIZE
    cols = q.shape[1] // kv_heads
    group = cols // size
    scaling = size ** (-0.5)
    every = range(kv_heads)

    def peer(d):
        return lax.rem(c + d, ctxs)

    def partner(e):
        return lax.rem(p + e, pairs)

    loads = {}

    def load(h, index, src, dst):
        copy = pltpu.make_async_copy(src, dst, load_sem.at[h, index])
        copy.start()
        loads[h, index] = copy

    for h in every:
        narrow = pl.ds(h * size, size)
        load(h, 0, kp.at[:, narrow], gp.at[h, own, 0])
        load(h, 1, vp.at[:, narrow], gp.at[h, own, 1])
        load(h, 2, kr.at[0, :, narrow], gr.at[h, c, 0])
        load(h, 3, vr.at[0, :, narrow], gr.at[h, c, 1])
    for h in every:
        wide = pl.ds(h * cols, cols)
        load(h, 4, q.at[:, wide], q_v.at[h])
        load(h, 5, do.at[:, wide], do_v.at[h])
        load(h, 6, aq.at[0, :, wide], aq_v.at[h])
        load(h, 7, ado.at[0, :, wide], ado_v.at[h])
    greet(pairs, ctxs, p, c)

    across = {h: [] for h in every}
    replies = {h: [] for h in every}
    forwards = {h: [] for h in every}
    for h in every:
        for i in range(4):
            loads[h, i].wait()
        for d in range(1, ctxs):
            own_slot = gp.at[h, own]
            across[h].append(
                remote(own_slot, own_slot, g_send.at[h, d - 1], g_recv.at[h, d - 1], {"ctx": peer(d)})
            )
        for e in range(1, pairs):
            own_slot = gp.at[h, own]
            forwards[h].append(
                remote(own_slot, own_slot, f_send.at[h, e - 1, 0], f_recv.at[h, e - 1, 0], {"pair": partner(e)})
            )
        for d in range(1, ctxs):
            reply = gr.at[h, c]
            replies[h].append(
                remote(reply, reply, r_send.at[h, d - 1], r_recv.at[h, d - 1], {"ctx": peer(d)})
            )

    def forward(h):
        for d in range(1, ctxs):
            across[h][d - 1].wait_recv()
            slot = gp.at[h, p * ctxs + lax.rem(c + ctxs - d, ctxs)]
            for e in range(1, pairs):
                forwards[h].append(
                    remote(slot, slot, f_send.at[h, e - 1, d], f_recv.at[h, e - 1, d], {"pair": partner(e)})
                )

    inner = {h: [] for h in every}
    outer = {h: [] for h in every}
    back = {h: [] for h in every}

    def send_terms(h):
        for d in list(range(1, ctxs)) + [0]:
            for e in range(1, pairs):
                inner[h].append((d, remote(
                    tp.at[h, partner(e) * ctxs + peer(d)], from_pair.at[h, e - 1, d],
                    x_send.at[h, e - 1, d], x_recv.at[h, e - 1, d], {"pair": partner(e)},
                )))
        for d in range(1, ctxs):
            back[h].append(remote(
                tr.at[h, peer(d)], from_reply.at[h, d - 1],
                z_send.at[h, d - 1], z_recv.at[h, d - 1], {"ctx": peer(d)},
            ))

    def pair_sum(h, d):
        total = tp[h, p * ctxs + peer(d)].astype(F32)
        for e in range(1, pairs):
            total = total + from_pair[h, e - 1, d].astype(F32)
        return total

    def pass_on(h):
        for d in range(1, ctxs):
            for at, copy in inner[h]:
                if at == d:
                    copy.wait_recv()
            summed[h, d - 1] = pair_sum(h, d).astype(BF16)
            outer[h].append(remote(
                summed.at[h, d - 1], from_ctx.at[h, d - 1],
                y_send.at[h, d - 1], y_recv.at[h, d - 1], {"ctx": peer(d)},
            ))

    stores = []

    def store(h, index, src, dst):
        copy = pltpu.make_async_copy(src, dst, store_sem.at[h, index])
        copy.start()
        stores.append(copy)

    def finish(h):
        narrow = pl.ds(h * size, size)
        for copy in back[h]:
            copy.wait_recv()
        total = tr[h, c].astype(F32)
        for d in range(1, ctxs):
            total = total + from_reply[h, d - 1].astype(F32)
        done_r[h] = total.astype(BF16)
        store(h, 4, done_r.at[h, 0], dkr.at[0, :, narrow])
        store(h, 5, done_r.at[h, 1], dvr.at[0, :, narrow])
        for at, copy in inner[h]:
            if at == 0:
                copy.wait_recv()
        total = pair_sum(h, 0)
        for d in range(1, ctxs):
            outer[h][d - 1].wait_recv()
            total = total + from_ctx[h, d - 1].astype(F32)
        done_p[h] = total.astype(BF16)
        store(h, 6, done_p.at[h, 0], dkp.at[:, narrow])
        store(h, 7, done_p.at[h, 1], dvp.at[:, narrow])

    prompt_len = plen[0]
    answer_len = alen[p]
    prompt_first = own * rows
    answer_first = c * later

    def stacked(ref, h, heads):
        return jnp.concatenate([ref[h, :, i * size : (i + 1) * size] for i in heads], axis=0)

    forward(0)
    for h in every:
        for copy in forwards[h] + replies[h]:
            copy.wait_recv()
        keys = gp[h, :, 0].reshape(slots * rows, size)
        values = gp[h, :, 1].reshape(slots * rows, size)
        keys_r = gr[h, :, 0].reshape(ctxs * later, size)
        values_r = gr[h, :, 1].reshape(ctxs * later, size)
        keys_t, values_t = keys.T, values.T
        keys_rt, values_rt = keys_r.T, values_r.T
        for i in range(4, 8):
            loads[h, i].wait()
        for answer in (False, True):
            count = later if answer else rows
            per_block = max(1, 256 // count)
            first = answer_first if answer else prompt_first
            live = answer_len if answer else prompt_len
            for start in range(0, group, per_block):
                heads = list(range(start, min(group, start + per_block)))
                lanes = len(heads) * count
                pos = row_positions(first, lanes, count)
                queries = stacked(aq_v if answer else q_v, h, heads)
                cotangent = stacked(ado_v if answer else do_v, h, heads)
                live_row = (
                    first
                    + lax.rem(lax.broadcasted_iota(jnp.int32, cotangent.shape, 0), jnp.int32(count))
                    < live
                )
                cotangent = jnp.where(live_row, cotangent.astype(F32), 0.0).astype(BF16)
                limit = jnp.minimum(pos, live - 1)
                if answer:
                    whole = jnp.full((1, lanes), prompt_len - 1, jnp.int32)
                    parts = [
                        (keys, values, keys_t, values_t, whole),
                        (keys_r, values_r, keys_rt, values_rt, limit),
                    ]
                    grads = [(kgrad, vgrad, False), (kgrad_r, vgrad_r, start == 0)]
                else:
                    parts = [(keys, values, keys_t, values_t, limit)]
                    grads = [(kgrad, vgrad, start == 0)]
                o, g = attend_block(parts, queries, cotangent, pos < live, scaling, grads)
                o, g = o.T, g.T
                for i, k in enumerate(heads):
                    cut, at = slice(i * count, (i + 1) * count), slice(k * size, (k + 1) * size)
                    (aout_v if answer else out_v)[h, :, at] = o[cut]
                    (adq_v if answer else dq_v)[h, :, at] = g[cut]
                if not answer and start == 0:
                    if h > 0:
                        pass_on(h - 1)
                    if h + 1 < kv_heads:
                        forward(h + 1)
        tp[h, :, 0] = (kgrad[...] * scaling).astype(BF16).reshape(slots, rows, size)
        tp[h, :, 1] = vgrad[...].astype(BF16).reshape(slots, rows, size)
        tr[h, :, 0] = (kgrad_r[...] * scaling).astype(BF16).reshape(ctxs, later, size)
        tr[h, :, 1] = vgrad_r[...].astype(BF16).reshape(ctxs, later, size)
        send_terms(h)
        wide = pl.ds(h * cols, cols)
        store(h, 0, out_v.at[h], out.at[:, wide])
        store(h, 1, dq_v.at[h], dq.at[:, wide])
        store(h, 2, aout_v.at[h], aout.at[0, :, wide])
        store(h, 3, adq_v.at[h], adq.at[0, :, wide])
        if h > 0:
            finish(h - 1)
    pass_on(kv_heads - 1)
    finish(kv_heads - 1)
    for h in every:
        for copy in across[h] + forwards[h] + replies[h] + outer[h] + back[h]:
            copy.wait_send()
        for _, copy in inner[h]:
            copy.wait_send()
    for copy in stores:
        copy.wait()


def fused(pairs, ctxs, q, kp, vp, aq, kr, vr, do, ado, plen, alen):
    size = HEAD_SIZE
    rows, width = kp.shape
    later = kr.shape[1]
    heads = width // size
    cols = q.shape[1] // heads
    slots = pairs * ctxs
    smem = pl.BlockSpec(memory_space=pltpu.SMEM)
    hbm = pl.BlockSpec(memory_space=pltpu.HBM)
    dma = pltpu.SemaphoreType.DMA
    like = lambda x: jax.ShapeDtypeStruct(x.shape, BF16)
    wide = pltpu.VMEM((heads, rows, cols), BF16)
    wide_r = pltpu.VMEM((heads, later, cols), BF16)
    terms = pltpu.VMEM((heads, slots, 2, rows, size), BF16)
    terms_r = pltpu.VMEM((heads, ctxs, 2, later, size), BF16)
    return pl.pallas_call(
        functools.partial(fused_kernel, pairs, ctxs, heads),
        out_shape=tuple(map(like, (q, aq, q, kp, vp, aq, kr, vr))),
        in_specs=[smem] * 2 + [hbm] * 8,
        out_specs=(hbm,) * 8,
        scratch_shapes=[
            terms, terms_r, wide, wide_r, wide, wide_r, wide, wide_r, wide, wide_r,
            pltpu.VMEM((slots * rows, size), F32),
            pltpu.VMEM((slots * rows, size), F32),
            pltpu.VMEM((ctxs * later, size), F32),
            pltpu.VMEM((ctxs * later, size), F32),
            terms, terms_r,
            pltpu.VMEM((heads, pairs - 1, ctxs, 2, rows, size), BF16),
            pltpu.VMEM((heads, ctxs - 1, 2, rows, size), BF16),
            pltpu.VMEM((heads, ctxs - 1, 2, later, size), BF16),
            pltpu.VMEM((heads, ctxs - 1, 2, rows, size), BF16),
            pltpu.VMEM((heads, 2, rows, size), BF16),
            pltpu.VMEM((heads, 2, later, size), BF16),
            dma((heads, 8)), dma((heads, 8)),
            dma((heads, ctxs - 1)), dma((heads, ctxs - 1)),
            dma((heads, ctxs - 1)), dma((heads, ctxs - 1)),
            dma((heads, pairs - 1, ctxs)), dma((heads, pairs - 1, ctxs)),
            dma((heads, pairs - 1, ctxs)), dma((heads, pairs - 1, ctxs)),
            dma((heads, ctxs - 1)), dma((heads, ctxs - 1)),
            dma((heads, ctxs - 1)), dma((heads, ctxs - 1)),
        ],
        compiler_params=pltpu.CompilerParams(
            collective_id=0, has_side_effects=True, vmem_limit_bytes=56 * 2**20
        ),
    )(plen, alen, q, kp, vp, aq, kr, vr, do, ado)


def hand_on_kernel(count, *refs):
    sems = refs[-1]
    copies = [
        pltpu.make_async_copy(refs[i], refs[count + i], sems.at[i]) for i in range(count)
    ]
    for copy in copies:
        copy.start()
    for copy in copies:
        copy.wait()


def hand_on(arrays):
    hbm = pl.BlockSpec(memory_space=pltpu.HBM)
    count = len(arrays)
    return pl.pallas_call(
        functools.partial(hand_on_kernel, count),
        out_shape=tuple(jax.ShapeDtypeStruct(x.shape, x.dtype) for x in arrays),
        in_specs=[hbm] * count,
        out_specs=(hbm,) * count,
        scratch_shapes=[pltpu.SemaphoreType.DMA((count,))],
    )(*arrays)


def body(pairs, ctxs, *operands):
    return hand_on(fused(pairs, ctxs, *operands))


def solution(mesh):
    flat = P(("pair", "ctx"), "head")
    deep = P("pair", "ctx", "head")
    return jax.shard_map(
        functools.partial(body, mesh.shape["pair"], mesh.shape["ctx"]),
        mesh=mesh,
        in_specs=(flat, flat, flat, deep, deep, deep, flat, deep, P(), P()),
        out_specs=(flat, deep, flat, flat, flat, deep, deep, deep),
        check_vma=False,
    )
```

time: 40.6 us -> 63.8 us (1.57)
  Pallas kernels: 29.8 us -> 62.4 us
  local copies, waits for them, and re-layouts: 8.96 us -> 0 us
    pallas_call x3 -> x2, Pallas kernels: 29.8 us -> 62.4 us  [the longest x1 36.9 us: hand_on(): pl.pallas_call(functools.partial(hand_on_kernel, count), out_shape=tuple(...]
    unnamed x20 -> x0, local copies, waits for them, and re-layouts: 8.96 us -> none
where the time goes in v2:
time: 63.8 us; the launch traced here: 63.7 us
  Pallas kernels  62.4 us (98%)
  between operations  1.29 us (2%)
    pallas_call x1, Pallas kernels, hand_on(): pl.pallas_call(functools.partial(hand_on_kernel, count), out_shape=tuple(...  36.9 us
    pallas_call x1, Pallas kernels, fused(): pl.pallas_call(functools.partial(fused_kernel, pairs, ctxs, heads), out_s...  25.5 us

profile of v2, /device:TPU:0, one launch (start us, length us, event | category | flops | bytes accessed | tf_op | source)
XLA Modules:
  0.0 63.7 jit_solution(14485437441707261740)
XLA Ops:
  1.3 25.5 %shard_map.161 = (bf16[64,2048]{1,0:T(8,128)(2,1)}, bf16[1,64,2048]{2,1,0:T(8,128)(2,1)}, bf16[64,2048]{1,0:T(8,128)(2,1)}, bf16[64,256]{1,0:T(8,128)(2,1)}, bf1...) custom-call(s32[1]{0:T(128)S(6)} %copy.18.plen, ...), custom_call_target="tpu_custom_call" | custom-call | tf_op jit(solution)/shard_map/pallas_call | solution.py:324
  26.8 36.9 %shard_map.162 = (bf16[64,2048]{1,0:T(8,128)(2,1)}, bf16[1,64,2048]{2,1,0:T(8,128)(2,1)}, bf16[64,2048]{1,0:T(8,128)(2,1)}, bf16[64,256]{1,0:T(8,128)(2,1)}, bf1...) custom-call(bf16[64,2048]{1,0:T(8,128)(2,1)} %get-tuple-element.16.r, ...), custom_call_target="tpu_custom_call" | custom-call | tf_op jit(solution)/shard_map/pallas_call | solution.py:370

commit v3 on v2

--- a/solution.py
+++ b/solution.py
@@ -88,9 +88,10 @@
 def fused_kernel(
     pairs, ctxs, kv_heads,
     plen, alen, q, kp, vp, aq, kr, vr, do, ado,
+    out_h, aout_h, dq_h, dkp_h, dvp_h, adq_h, dkr_h, dvr_h,
+    gp, gr, q_v, aq_v, do_v, ado_v,
     out, aout, dq, dkp, dvp, adq, dkr, dvr,
-    gp, gr, q_v, aq_v, do_v, ado_v, out_v, aout_v, dq_v, adq_v,
-    kgrad, vgrad, kgrad_r, vgrad_r, tp, tr, from_pair, from_ctx, from_reply, summed, done_p, done_r,
+    kgrad, vgrad, kgrad_r, vgrad_r, tp, tr, from_pair, from_ctx, from_reply, summed,
     load_sem, store_sem,
     g_send, g_recv, r_send, r_recv, f_send, f_recv,
     x_send, x_recv, y_send, y_recv, z_send, z_recv,
@@ -134,21 +135,20 @@
     across = {h: [] for h in every}
     replies = {h: [] for h in every}
     forwards = {h: [] for h in every}
-    for h in every:
+
+    def send_keys(h):
         for i in range(4):
             loads[h, i].wait()
-        for d in range(1, ctxs):
-            own_slot = gp.at[h, own]
+        own_slot, reply = gp.at[h, own], gr.at[h, c]
+        for d in range(1, ctxs):
             across[h].append(
                 remote(own_slot, own_slot, g_send.at[h, d - 1], g_recv.at[h, d - 1], {"ctx": peer(d)})
             )
         for e in range(1, pairs):
-            own_slot = gp.at[h, own]
             forwards[h].append(
                 remote(own_slot, own_slot, f_send.at[h, e - 1, 0], f_recv.at[h, e - 1, 0], {"pair": partner(e)})
             )
         for d in range(1, ctxs):
-            reply = gr.at[h, c]
             replies[h].append(
                 remote(reply, reply, r_send.at[h, d - 1], r_recv.at[h, d - 1], {"ctx": peer(d)})
             )
@@ -173,6 +173,10 @@
                     tp.at[h, partner(e) * ctxs + peer(d)], from_pair.at[h, e - 1, d],
                     x_send.at[h, e - 1, d], x_recv.at[h, e - 1, d], {"pair": partner(e)},
                 )))
+
+    def send_replies(h):
+        tr[h, :, 0] = (kgrad_r[...] * scaling).astype(BF16).reshape(ctxs, later, size)
+        tr[h, :, 1] = vgrad_r[...].astype(BF16).reshape(ctxs, later, size)
         for d in range(1, ctxs):
             back[h].append(remote(
                 tr.at[h, peer(d)], from_reply.at[h, d - 1],
@@ -204,15 +208,17 @@
         stores.append(copy)
 
     def finish(h):
-        narrow = pl.ds(h * size, size)
+        narrow = slice(h * size, (h + 1) * size)
         for copy in back[h]:
             copy.wait_recv()
         total = tr[h, c].astype(F32)
         for d in range(1, ctxs):
             total = total + from_reply[h, d - 1].astype(F32)
-        done_r[h] = total.astype(BF16)
-        store(h, 4, done_r.at[h, 0], dkr.at[0, :, narrow])
-        store(h, 5, done_r.at[h, 1], dvr.at[0, :, narrow])
+        dkr[0, :, narrow] = total[0].astype(BF16)
+        dvr[0, :, narrow] = total[1].astype(BF16)
+        cut = pl.ds(h * size, size)
+        store(h, 4, dkr.at[0, :, cut], dkr_h.at[0, :, cut])
+        store(h, 5, dvr.at[0, :, cut], dvr_h.at[0, :, cut])
         for at, copy in inner[h]:
             if at == 0:
                 copy.wait_recv()
@@ -220,9 +226,10 @@
         for d in range(1, ctxs):
             outer[h][d - 1].wait_recv()
             total = total + from_ctx[h, d - 1].astype(F32)
-        done_p[h] = total.astype(BF16)
-        store(h, 6, done_p.at[h, 0], dkp.at[:, narrow])
-        store(h, 7, done_p.at[h, 1], dvp.at[:, narrow])
+        dkp[:, narrow] = total[0].astype(BF16)
+        dvp[:, narrow] = total[1].astype(BF16)
+        store(h, 6, dkp.at[:, cut], dkp_h.at[:, cut])
+        store(h, 7, dvp.at[:, cut], dvp_h.at[:, cut])
 
     prompt_len = plen[0]
     answer_len = alen[p]
@@ -232,19 +239,27 @@
     def stacked(ref, h, heads):
         return jnp.concatenate([ref[h, :, i * size : (i + 1) * size] for i in heads], axis=0)
 
+    send_keys(0)
     forward(0)
+    for h in range(1, kv_heads):
+        send_keys(h)
     for h in every:
-        for copy in forwards[h] + replies[h]:
+        last = h + 1 == kv_heads
+        for copy in forwards[h]:
             copy.wait_recv()
         keys = gp[h, :, 0].reshape(slots * rows, size)
         values = gp[h, :, 1].reshape(slots * rows, size)
-        keys_r = gr[h, :, 0].reshape(ctxs * later, size)
-        values_r = gr[h, :, 1].reshape(ctxs * later, size)
         keys_t, values_t = keys.T, values.T
-        keys_rt, values_rt = keys_r.T, values_r.T
         for i in range(4, 8):
             loads[h, i].wait()
-        for answer in (False, True):
+        fresh = True
+        for answer in (True, False) if last else (False, True):
+            if answer:
+                for copy in replies[h]:
+                    copy.wait_recv()
+                keys_r = gr[h, :, 0].reshape(ctxs * later, size)
+                values_r = gr[h, :, 1].reshape(ctxs * later, size)
+                keys_rt, values_rt = keys_r.T, values_r.T
             count = later if answer else rows
             per_block = max(1, 256 // count)
             first = answer_first if answer else prompt_first
@@ -268,31 +283,37 @@
                         (keys, values, keys_t, values_t, whole),
                         (keys_r, values_r, keys_rt, values_rt, limit),
                     ]
-                    grads = [(kgrad, vgrad, False), (kgrad_r, vgrad_r, start == 0)]
+                    grads = [(kgrad, vgrad, fresh), (kgrad_r, vgrad_r, start == 0)]
                 else:
                     parts = [(keys, values, keys_t, values_t, limit)]
-                    grads = [(kgrad, vgrad, start == 0)]
+                    grads = [(kgrad, vgrad, fresh)]
                 o, g = attend_block(parts, queries, cotangent, pos < live, scaling, grads)
                 o, g = o.T, g.T
                 for i, k in enumerate(heads):
-                    cut, at = slice(i * count, (i + 1) * count), slice(k * size, (k + 1) * size)
-                    (aout_v if answer else out_v)[h, :, at] = o[cut]
-                    (adq_v if answer else dq_v)[h, :, at] = g[cut]
-                if not answer and start == 0:
+                    cut = slice(i * count, (i + 1) * count)
+                    at = slice(h * cols + k * size, h * cols + (k + 1) * size)
+                    if answer:
+                        aout[0, :, at] = o[cut]
+                        adq[0, :, at] = g[cut]
+                    else:
+                        out[:, at] = o[cut]
+                        dq[:, at] = g[cut]
+                if fresh:
                     if h > 0:
                         pass_on(h - 1)
-                    if h + 1 < kv_heads:
+                    if not last:
                         forward(h + 1)
+                fresh = False
+            if answer:
+                send_replies(h)
         tp[h, :, 0] = (kgrad[...] * scaling).astype(BF16).reshape(slots, rows, size)
         tp[h, :, 1] = vgrad[...].astype(BF16).reshape(slots, rows, size)
-        tr[h, :, 0] = (kgrad_r[...] * scaling).astype(BF16).reshape(ctxs, later, size)
-        tr[h, :, 1] = vgrad_r[...].astype(BF16).reshape(ctxs, later, size)
         send_terms(h)
         wide = pl.ds(h * cols, cols)
-        store(h, 0, out_v.at[h], out.at[:, wide])
-        store(h, 1, dq_v.at[h], dq.at[:, wide])
-        store(h, 2, aout_v.at[h], aout.at[0, :, wide])
-        store(h, 3, adq_v.at[h], adq.at[0, :, wide])
+        store(h, 0, out.at[:, wide], out_h.at[:, wide])
+        store(h, 1, dq.at[:, wide], dq_h.at[:, wide])
+        store(h, 2, aout.at[0, :, wide], aout_h.at[0, :, wide])
+        store(h, 3, adq.at[0, :, wide], adq_h.at[0, :, wide])
         if h > 0:
             finish(h - 1)
     pass_on(kv_heads - 1)
@@ -327,7 +348,8 @@
         in_specs=[smem] * 2 + [hbm] * 8,
         out_specs=(hbm,) * 8,
         scratch_shapes=[
-            terms, terms_r, wide, wide_r, wide, wide_r, wide, wide_r, wide, wide_r,
+            terms, terms_r, wide, wide_r, wide, wide_r,
+            *[pltpu.VMEM(x.shape, BF16) for x in (q, aq, q, kp, vp, aq, kr, vr)],
             pltpu.VMEM((slots * rows, size), F32),
             pltpu.VMEM((slots * rows, size), F32),
             pltpu.VMEM((ctxs * later, size), F32),
@@ -337,8 +359,6 @@
             pltpu.VMEM((heads, ctxs - 1, 2, rows, size), BF16),
             pltpu.VMEM((heads, ctxs - 1, 2, later, size), BF16),
             pltpu.VMEM((heads, ctxs - 1, 2, rows, size), BF16),
-            pltpu.VMEM((heads, 2, rows, size), BF16),
-            pltpu.VMEM((heads, 2, later, size), BF16),
             dma((heads, 8)), dma((heads, 8)),
             dma((heads, ctxs - 1)), dma((heads, ctxs - 1)),
             dma((heads, ctxs - 1)), dma((heads, ctxs - 1)),
@@ -354,13 +374,16 @@
 
 
 def hand_on_kernel(count, *refs):
+    sources, targets, held = refs[:count], refs[count : 2 * count], refs[2 * count : 3 * count]
     sems = refs[-1]
-    copies = [
-        pltpu.make_async_copy(refs[i], refs[count + i], sems.at[i]) for i in range(count)
-    ]
-    for copy in copies:
+    ins = [pltpu.make_async_copy(sources[i], held[i], sems.at[0, i]) for i in range(count)]
+    outs = [pltpu.make_async_copy(held[i], targets[i], sems.at[1, i]) for i in range(count)]
+    for copy in ins:
         copy.start()
-    for copy in copies:
+    for i in range(count):
+        ins[i].wait()
+        outs[i].start()
+    for copy in outs:
         copy.wait()
 
 
@@ -372,7 +395,9 @@
         out_shape=tuple(jax.ShapeDtypeStruct(x.shape, x.dtype) for x in arrays),
         in_specs=[hbm] * count,
         out_specs=(hbm,) * count,
-        scratch_shapes=[pltpu.SemaphoreType.DMA((count,))],
+        scratch_shapes=[pltpu.VMEM(x.shape, x.dtype) for x in arrays]
+        + [pltpu.SemaphoreType.DMA((2, count))],
+        compiler_params=pltpu.CompilerParams(vmem_limit_bytes=56 * 2**20),
     )(*arrays)
 
 

time: 63.8 us -> 29.4 us (0.46)
  Pallas kernels: 62.4 us -> 27.9 us
    pallas_call x1, Pallas kernels: 36.9 us -> 2.08 us  [hand_on(): pl.pallas_call(functools.partial(hand_on_kernel, count), out_shape=tuple(...]
where the time goes in v3:
time: 29.4 us; the launch traced here: 29.2 us
  Pallas kernels  27.9 us (95%)
  between operations  1.29 us (4%)
    pallas_call x1, Pallas kernels, fused(): pl.pallas_call(functools.partial(fused_kernel, pairs, ctxs, heads), out_s...  25.9 us
    pallas_call x1, Pallas kernels, hand_on(): pl.pallas_call(functools.partial(hand_on_kernel, count), out_shape=tuple(...  2.08 us

profile of v3, /device:TPU:0, one launch (start us, length us, event | category | flops | bytes accessed | tf_op | source)
XLA Modules:
  0.0 29.2 jit_solution(10843095557294937864)
XLA Ops:
  1.3 25.9 %shard_map.161 = (bf16[64,2048]{1,0:T(8,128)(2,1)}, bf16[1,64,2048]{2,1,0:T(8,128)(2,1)}, bf16[64,2048]{1,0:T(8,128)(2,1)}, bf16[64,256]{1,0:T(8,128)(2,1)}, bf1...) custom-call(s32[1]{0:T(128)S(6)} %copy.18.plen, ...), custom_call_target="tpu_custom_call" | custom-call | tf_op jit(solution)/shard_map/pallas_call | solution.py:345
  27.1 2.1 %shard_map.162 = (bf16[64,2048]{1,0:T(8,128)(2,1)}, bf16[1,64,2048]{2,1,0:T(8,128)(2,1)}, bf16[64,2048]{1,0:T(8,128)(2,1)}, bf16[64,256]{1,0:T(8,128)(2,1)}, bf1...) custom-call(bf16[64,2048]{1,0:T(8,128)(2,1)} %get-tuple-element.16.r, ...), custom_call_target="tpu_custom_call" | custom-call | tf_op jit(solution)/shard_map/pallas_call | solution.py:393

commit v4 on v3

--- a/solution.py
+++ b/solution.py
@@ -42,8 +42,7 @@
     return first + lax.rem(lane, jnp.int32(rows))
 
 
-def attend_block(parts, queries, cotangent, valid, scaling, grads):
-    factor = scaling * math.log2(math.e)
+def first_products(parts, queries, cotangent):
     scores = []
     top = None
     for keys, _, _, _, limit in parts:
@@ -53,12 +52,17 @@
         m = jnp.max(s, axis=0, keepdims=True)
         top = m if top is None else jnp.maximum(top, m)
         scores.append(s)
+    return scores, top, [dot_nt(part[1], cotangent) for part in parts]
+
+
+def attend_block(parts, queries, cotangent, valid, scaling, grads, products):
+    factor = scaling * math.log2(math.e)
+    scores, top, prob_grads = products
     terms = [jnp.exp2((s - top) * factor) for s in scores]
     total = sum(jnp.sum(t, axis=0, keepdims=True) for t in terms)
     inverse = 1.0 / total
     output = sum(dot(part[3], t.astype(BF16)) for part, t in zip(parts, terms))
     output = jnp.where(valid, output * inverse, 0.0).astype(BF16)
-    prob_grads = [dot_nt(part[1], cotangent) for part in parts]
     shares = [t * inverse for t in terms]
     delta = sum(jnp.sum(w * g, axis=0, keepdims=True) for w, g in zip(shares, prob_grads))
     query_grad = None
@@ -254,6 +258,7 @@
             loads[h, i].wait()
         fresh = True
         for answer in (True, False) if last else (False, True):
+            blocks = []
             if answer:
                 for copy in replies[h]:
                     copy.wait_recv()
@@ -264,18 +269,12 @@
             per_block = max(1, 256 // count)
             first = answer_first if answer else prompt_first
             live = answer_len if answer else prompt_len
+            live_row = first + lax.broadcasted_iota(jnp.int32, (count, size), 0) < live
+            q_ref, do_ref = (aq_v, ado_v) if answer else (q_v, do_v)
             for start in range(0, group, per_block):
                 heads = list(range(start, min(group, start + per_block)))
                 lanes = len(heads) * count
                 pos = row_positions(first, lanes, count)
-                queries = stacked(aq_v if answer else q_v, h, heads)
-                cotangent = stacked(ado_v if answer else do_v, h, heads)
-                live_row = (
-                    first
-                    + lax.rem(lax.broadcasted_iota(jnp.int32, cotangent.shape, 0), jnp.int32(count))
-                    < live
-                )
-                cotangent = jnp.where(live_row, cotangent.astype(F32), 0.0).astype(BF16)
                 limit = jnp.minimum(pos, live - 1)
                 if answer:
                     whole = jnp.full((1, lanes), prompt_len - 1, jnp.int32)
@@ -283,11 +282,33 @@
                         (keys, values, keys_t, values_t, whole),
                         (keys_r, values_r, keys_rt, values_rt, limit),
                     ]
-                    grads = [(kgrad, vgrad, fresh), (kgrad_r, vgrad_r, start == 0)]
                 else:
                     parts = [(keys, values, keys_t, values_t, limit)]
-                    grads = [(kgrad, vgrad, fresh)]
-                o, g = attend_block(parts, queries, cotangent, pos < live, scaling, grads)
+                blocks.append((start, heads, pos, parts))
+
+            def begin(index):
+                _, heads, _, parts = blocks[index]
+                queries = stacked(q_ref, h, heads)
+                cotangent = jnp.concatenate(
+                    [
+                        jnp.where(live_row, do_ref[h, :, i * size : (i + 1) * size].astype(F32), 0.0)
+                        for i in heads
+                    ],
+                    axis=0,
+                ).astype(BF16)
+                return queries, cotangent, first_products(parts, queries, cotangent)
+
+            ahead = begin(0)
+            for index, (start, heads, pos, parts) in enumerate(blocks):
+                queries, cotangent, products = ahead
+                if index + 1 < len(blocks):
+                    ahead = begin(index + 1)
+                grads = [(kgrad, vgrad, fresh)]
+                if answer:
+                    grads.append((kgrad_r, vgrad_r, start == 0))
+                o, g = attend_block(
+                    parts, queries, cotangent, pos < live, scaling, grads, products
+                )
                 o, g = o.T, g.T
                 for i, k in enumerate(heads):
                     cut = slice(i * count, (i + 1) * count)

time: 29.4 us -> 28.7 us (0.976)
  Pallas kernels: 27.9 us -> 27.2 us
    pallas_call x1, Pallas kernels: 25.9 us -> 25.1 us  [fused(): pl.pallas_call(functools.partial(fused_kernel, pairs, ctxs, heads), out_s...]
where the time goes in v4:
time: 28.7 us; the launch traced here: 28.5 us
  Pallas kernels  27.2 us (95%)
  between operations  1.29 us (4%)
    pallas_call x1, Pallas kernels, fused(): pl.pallas_call(functools.partial(fused_kernel, pairs, ctxs, heads), out_s...  25.1 us
    pallas_call x1, Pallas kernels, hand_on(): pl.pallas_call(functools.partial(hand_on_kernel, count), out_shape=tuple(...  2.08 us

profile of v4, /device:TPU:0, one launch (start us, length us, event | category | flops | bytes accessed | tf_op | source)
XLA Modules:
  0.0 28.5 jit_solution(13263972619320335779)
XLA Ops:
  1.3 25.1 %shard_map.161 = (bf16[64,2048]{1,0:T(8,128)(2,1)}, bf16[1,64,2048]{2,1,0:T(8,128)(2,1)}, bf16[64,2048]{1,0:T(8,128)(2,1)}, bf16[64,256]{1,0:T(8,128)(2,1)}, bf1...) custom-call(s32[1]{0:T(128)S(6)} %copy.18.plen, ...), custom_call_target="tpu_custom_call" | custom-call | tf_op jit(solution)/shard_map/pallas_call | solution.py:366
  26.4 2.1 %shard_map.162 = (bf16[64,2048]{1,0:T(8,128)(2,1)}, bf16[1,64,2048]{2,1,0:T(8,128)(2,1)}, bf16[64,2048]{1,0:T(8,128)(2,1)}, bf16[64,256]{1,0:T(8,128)(2,1)}, bf1...) custom-call(bf16[64,2048]{1,0:T(8,128)(2,1)} %get-tuple-element.16.r, ...), custom_call_target="tpu_custom_call" | custom-call | tf_op jit(solution)/shard_map/pallas_call | solution.py:414
